TPU v7x, 32 devices: a whole 2x2x4 slice. The times are simulated.
32 devices in a mesh: sky: 8 (over z, y), visit: 4 (over x, core).
Axes of the slice: x: 2, y: 2, z: 4, core: 2. Of those that a mesh axis runs over, the one named last changes fastest.
Arguments:
- science: float32 [32, 512, 256], P('visit', 'sky'), may hold values from -6 to 6
- inv_variance: float32 [32, 512, 256], P('visit', 'sky'), may hold values from 0.3 to 3
- psf_kernel: float32 [11, 11], replicated, may hold values from 0.01 to 0.12
- offsets: int32 [32, 16], replicated, may hold values from -2 to 2, as said below
Outputs:
- likelihood: float32 [16, 512, 256], P(None, ('sky', 'visit'))
Inputs may be any that keep to these rules, and one draw needn't show every extreme that they name: offsets[0, k] is 0 for every velocity; offsets[31, 0] is 2 and offsets[31, 1] is -2.
All inputs are finite; a program needn't handle non-finite values.
Results may differ from a plain program's by a relative error of at most 0.0001.
Values sent between devices are 32-bit elements; how exact they have to be, the bound alone decides.
A program may use at most 64 MiB of HBM per device.

v0:
```python
import jax
import jax.numpy as jnp
from jax import lax
from jax.sharding import PartitionSpec as P

BR = 8
MAXOFF = 2


def padded_2(block, sides, width):
    for axis, dim in sides:
        count = lax.axis_size(axis)
        forward = [(i, i + 1) for i in range(count - 1)]
        backward = [(target, source) for source, target in forward]
        low = lax.ppermute(
            lax.slice_in_dim(block, block.shape[dim] - width, None, axis=dim), axis, forward
        )
        high = lax.ppermute(lax.slice_in_dim(block, 0, width, axis=dim), axis, backward)
        block = jnp.concatenate([low, block, high], axis=dim)
    return block


def correlate(bordered, psf_kernel, radius):
    kernel_size = 2 * radius + 1
    row_count = bordered.shape[2] - 2 * radius
    col_count = bordered.shape[3]
    weights = jnp.stack([psf_kernel, psf_kernel * psf_kernel])
    padded = jnp.pad(bordered, ((0, 0), (0, 0), (0, 0), (radius, radius)))
    running = jnp.zeros((bordered.shape[0], bordered.shape[1], row_count, col_count), jnp.float32)
    for row_tap in range(kernel_size):
        for col_tap in range(kernel_size):
            running = (
                running
                + weights[:, row_tap, col_tap][:, None, None, None]
                * padded[:, :, row_tap : row_tap + row_count, col_tap : col_tap + col_count]
            )
    return running


def stack_shifted(padded, visit_offsets, reach_rows, row_count):
    stacked = jnp.zeros((2, visit_offsets.shape[1], row_count, padded.shape[3]), jnp.float32)
    for offset_value in range(-MAXOFF, MAXOFF + 1):
        onehot = (visit_offsets == offset_value).astype(jnp.float32)
        start_row = reach_rows + offset_value * BR
        window = padded[:, :, start_row : start_row + row_count, :]
        stacked = stacked + jnp.einsum(
            "tk,ctrw->ckrw", onehot, window, precision=lax.Precision.HIGHEST
        )
    return stacked


def shards(science, inv_variance, psf_kernel, offsets):
    radius = (psf_kernel.shape[0] - 1) // 2
    paired = jnp.stack([science * inv_variance, inv_variance])
    bordered = padded_2(paired, (("sky", 2),), radius)
    images = correlate(bordered, psf_kernel, radius)
    reach_rows = MAXOFF * BR
    regrouped = lax.all_to_all(images, "visit", split_axis=2, concat_axis=1, tiled=True)
    padded = padded_2(regrouped, ((("sky", "visit"), 2),), reach_rows)
    stacked = stack_shifted(padded, offsets, reach_rows, regrouped.shape[2])
    return stacked[0] / jnp.sqrt(stacked[1])


def solution(mesh):
    return jax.shard_map(
        shards,
        mesh=mesh,
        in_specs=(P("visit", "sky", None), P("visit", "sky", None), P(), P()),
        out_specs=P(None, ("sky", "visit"), None),
        check_vma=False,
    )
```

profile of v0, /device:TPU:1, one launch (start us, length us, event | category | flops | bytes accessed | tf_op | source)
XLA Modules:
  0.0 90.2 jit_solution(16747805909025785455)
XLA Ops:
  0.0 0.0 copy-start
  0.0 1.8 %copy_bitcast_fusion.1 = (f32[1,8,64,256]{3,1,0,2:T(8,128)S(1)}, f32[1,8,64,256]{3,1,0,2:T(8,128)S(1)}) fusion(f32[8,64,256]{2,1,0:T(8,128)} %param.5, f32[8,64,256]{2,1,0:T(8,128)} %param.4), kind=kLoop, calls=%fused_computation.270 | loop fusion | flops 131072 | bytes 2097152 | tf_op jit(solution)/shard_map/stack | solution.py:54
  1.8 4.0 %collective-permute-start = (f32[2,8,5,256]{3,1,0,2:T(8,128)S(1)}, f32[2,8,5,256]{3,1,0,2:T(8,128)S(1)}, u32[]{:S(2)}, u32[]{:S(2)}) collective-permute-start(f32[2,8,5,256]{3,1,0,2:T(8,128)S(1)} %get-tuple-element.128), channel_id=1, source_target_pairs={{0,4},{4,8},{8,12},{12,16},{16,20},{20,24},{24,28},{1,5},{5,9},{9,... | collective-permute-start | bytes 245768 | tf_op jit(solution)/shard_map/ppermute | solution.py:15
  5.8 1.3 %collective-permute-start.1 = (f32[2,8,5,256]{3,1,0,2:T(8,128)S(1)}, f32[2,8,5,256]{3,1,0,2:T(8,128)S(1)}, u32[]{:S(2)}, u32[]{:S(2)}) collective-permute-start(f32[2,8,5,256]{3,1,0,2:T(8,128)S(1)} %get-tuple-element.129), channel_id=1, source_target_pairs={{4,0},{8,4},{12,8},{16,12},{20,16},{24,20},{28,24},{5,1},{9,5},{13... | collective-permute-start | bytes 245768 | tf_op jit(solution)/shard_map/ppermute | solution.py:18
  7.1 0.0 copy-done
  7.1 0.2 fusion.284
  7.3 0.2 fusion.392
  7.5 0.2 fusion.293
  7.7 0.2 fusion.356
  7.9 0.2 fusion.374
  8.1 0.2 fusion.365
  8.3 0.2 fusion.302
  8.5 0.2 fusion.347
  8.7 0.2 fusion.383
  8.8 0.2 fusion.311
  9.0 0.2 fusion.338
  9.2 0.2 fusion.320
  9.4 0.2 fusion.329
  9.6 0.2 fusion.401
  9.8 0.0 collective-permute-done
  9.8 1.2 %collective-permute-done.1 = f32[2,8,5,256]{3,1,0,2:T(8,128)S(1)} collective-permute-done((f32[2,8,5,256]{3,1,0,2:T(8,128)S(1)}, f32[2,8,5,256]{3,1,0,2:T(8,128)S(1)}, u32[]{:S(2)}, u32[]{:S(2)}) %collective-permute-start.1) | collective-permute-done | bytes 81952 | tf_op jit(solution)/shard_map/ppermute | solution.py:18
  11.0 0.5 select_maximum_fusion
  11.5 0.2 maximum_maximum_fusion
  11.7 29.4 %fusion.42 = f32[2,8,64,256]{3,1,0,2:T(8,128)S(1)} fusion(f32[2,8,74,266]{3,1,0,2:T(8,128)S(1)} %select_maximum_fusion, f32[2,8,69,256]{3,1,0,2:T(8,128)S(1)} %get-tuple-element.127, f32[1,8,64,256]{3,1,0,2:T(8,128)S(1)} %get-tuple-element.130, f32[1,8,64,256]{3,1,0,2:T(8,128)S(1)} %get-tuple-element.131, f32[2,8,69,256]{3,1,0,2:T(8,128)S(1)} %get-tuple-element.126, ...), kind=kLoop, calls=%fused_computation.50 | loop fusion | flops 63438848 | bytes 127927240 | tf_op jit(solution)/shard_map/add | solution.py:33
  41.1 0.0 copy-start.1
  41.1 18.1 %all_to_all.18 = f32[2,8,64,256]{3,1,0,2:T(8,128)S(1)} all-to-all(f32[2,8,64,256]{3,1,0,2:T(8,128)S(1)} %fusion.42), channel_id=1, replica_groups=mesh['sky'=8,'visit'=4] {'visit'}, dimensions={2} | all-to-all | bytes 2097152 | tf_op jit(solution)/shard_map/all_to_all | solution.py:58
  59.2 0.1 copy.26
  59.4 2.9 %collective-permute-start.3 = (f32[2,32,16,256]{3,1,2,0:T(8,128)S(1)}, f32[2,32,16,256]{3,1,2,0:T(8,128)S(1)}, u32[]{:S(2)}, u32[]{:S(2)}) collective-permute-start(f32[2,32,16,256]{3,1,2,0:T(8,128)S(1)} %bitcast.45), channel_id=1, source_target_pairs={{1,0},{2,1},{3,2},{4,3},{5,4},{6,5},{7,6},{8,7},{9,8},{10,9},{11,1... | collective-permute-start | bytes 3145736 | tf_op jit(solution)/shard_map/ppermute | solution.py:18
  62.3 2.6 %collective-permute-start.2 = (f32[2,32,16,256]{3,1,2,0:T(8,128)S(1)}, f32[2,32,16,256]{3,1,2,0:T(8,128)S(1)}, u32[]{:S(2)}, u32[]{:S(2)}) collective-permute-start(f32[2,32,16,256]{3,1,2,0:T(8,128)S(1)} %bitcast.46), channel_id=1, source_target_pairs={{0,1},{1,2},{2,3},{3,4},{4,5},{5,6},{6,7},{7,8},{8,9},{9,10},{10,1... | collective-permute-start | bytes 3145736 | tf_op jit(solution)/shard_map/ppermute | solution.py:15
  64.9 0.0 copy-done.1
  64.9 0.5 fusion.148
  65.4 17.1 %collective-permute-done.3 = f32[2,32,16,256]{3,1,2,0:T(8,128)S(1)} collective-permute-done((f32[2,32,16,256]{3,1,2,0:T(8,128)S(1)}, f32[2,32,16,256]{3,1,2,0:T(8,128)S(1)}, u32[]{:S(2)}, u32[]{:S(2)}) %collective-permute-start.3) | collective-permute-done | bytes 1048608 | tf_op jit(solution)/shard_map/ppermute | solution.py:18
  82.5 0.5 fusion.145
  83.0 4.9 %collective-permute-done.2 = f32[2,32,16,256]{3,1,2,0:T(8,128)S(1)} collective-permute-done((f32[2,32,16,256]{3,1,2,0:T(8,128)S(1)}, f32[2,32,16,256]{3,1,2,0:T(8,128)S(1)}, u32[]{:S(2)}, u32[]{:S(2)}) %collective-permute-start.2) | collective-permute-done | bytes 1048608 | tf_op jit(solution)/shard_map/ppermute | solution.py:15
  87.9 0.5 fusion
  88.4 0.5 fusion.18
  88.8 0.5 fusion.15
  89.4 0.9 copy.13
  (3 shorter events, 0.1 us)
Async XLA Ops:
  0.0 7.1 %copy-start = (f32[11,11]{1,0:T(8,128)S(1)}, f32[11,11]{1,0:T(8,128)}, u32[]{:S(2)}) copy-start(f32[11,11]{1,0:T(8,128)} %param.6) | copy-start | bytes 1456
  1.8 8.0 %collective-permute-start = (f32[2,8,5,256]{3,1,0,2:T(8,128)S(1)}, f32[2,8,5,256]{3,1,0,2:T(8,128)S(1)}, u32[]{:S(2)}, u32[]{:S(2)}) collective-permute-start(f32[2,8,5,256]{3,1,0,2:T(8,128)S(1)} %get-tuple-element.128), channel_id=1, source_target_pairs={{0,4},{4,8},{8,12},{12,16},{16,20},{20,24},{24,28},{1,5},{5,9},{9,... | collective-permute-start | bytes 245768 | tf_op jit(solution)/shard_map/ppermute | solution.py:15
  5.8 5.2 %collective-permute-start.1 = (f32[2,8,5,256]{3,1,0,2:T(8,128)S(1)}, f32[2,8,5,256]{3,1,0,2:T(8,128)S(1)}, u32[]{:S(2)}, u32[]{:S(2)}) collective-permute-start(f32[2,8,5,256]{3,1,0,2:T(8,128)S(1)} %get-tuple-element.129), channel_id=1, source_target_pairs={{4,0},{8,4},{12,8},{16,12},{20,16},{24,20},{28,24},{5,1},{9,5},{13... | collective-permute-start | bytes 245768 | tf_op jit(solution)/shard_map/ppermute | solution.py:18
  41.1 23.8 %copy-start.1 = (s32[32,16]{0,1:T(8,128)S(1)}, s32[32,16]{0,1:T(8,128)}, u32[]{:S(2)}) copy-start(s32[32,16]{0,1:T(8,128)} %param.7) | copy-start | bytes 6148
  59.4 23.2 %collective-permute-start.3 = (f32[2,32,16,256]{3,1,2,0:T(8,128)S(1)}, f32[2,32,16,256]{3,1,2,0:T(8,128)S(1)}, u32[]{:S(2)}, u32[]{:S(2)}) collective-permute-start(f32[2,32,16,256]{3,1,2,0:T(8,128)S(1)} %bitcast.45), channel_id=1, source_target_pairs={{1,0},{2,1},{3,2},{4,3},{5,4},{6,5},{7,6},{8,7},{9,8},{10,9},{11,1... | collective-permute-start | bytes 3145736 | tf_op jit(solution)/shard_map/ppermute | solution.py:18
  62.3 25.6 %collective-permute-start.2 = (f32[2,32,16,256]{3,1,2,0:T(8,128)S(1)}, f32[2,32,16,256]{3,1,2,0:T(8,128)S(1)}, u32[]{:S(2)}, u32[]{:S(2)}) collective-permute-start(f32[2,32,16,256]{3,1,2,0:T(8,128)S(1)} %bitcast.46), channel_id=1, source_target_pairs={{0,1},{1,2},{2,3},{3,4},{4,5},{5,6},{6,7},{7,8},{8,9},{9,10},{10,1... | collective-permute-start | bytes 3145736 | tf_op jit(solution)/shard_map/ppermute | solution.py:15
where the time goes:
time: 90.5 us; the launch traced here: 90.2 us
  other arithmetic  34.5 us (38%)
  waiting for transfers between devices  23.2 us (26%)
  blocking collectives  18.1 us (20%)
  starting transfers between devices  10.8 us (12%)
  matrix products  2.35 us (3%)
  local copies, waits for them, and re-layouts  1 us (1%)
    add x1, other arithmetic, correlate(): running + weights[:, row_tap, col_tap][:, None, None, None] * padded[:, :...  29.4 us
    ppermute x2, waiting for transfers between devices, padded_2(): lax.ppermute(lax.slice_in_dim(block, 0, width, axis=dim), axis, backward)  18.3 us
    all_to_all x1, blocking collectives, shards(): lax.all_to_all(images, 'visit', split_axis=2, concat_axis=1, tiled=True)  18.1 us
    ppermute x2, starting transfers between devices, padded_2(): lax.ppermute(lax.slice_in_dim(block, block.shape[dim] - width, None, axis...  6.59 us
    ppermute x2, waiting for transfers between devices, padded_2(): lax.ppermute(lax.slice_in_dim(block, block.shape[dim] - width, None, axis...  4.91 us
    ppermute x2, starting transfers between devices, padded_2(): lax.ppermute(lax.slice_in_dim(block, 0, width, axis=dim), axis, backward)  4.24 us
    slice x14, other arithmetic, correlate(): weights[:, row_tap, col_tap][:, None, None, None]  2.58 us
    dot_general x5, matrix products, stack_shifted(): jnp.einsum('tk,ctrw->ckrw', onehot, window, precision=lax.Precision.HIGHEST)  2.35 us
  transfers between devices with their start and end apart: 4, of which 3 were waited for; matrix products, arithmetic and copies ran while one was open for 4% of the time, Pallas kernels for 0%

commit v1 on v0

v1 whole, which is shorter than its diff:
```python
import jax
import jax.numpy as jnp
from jax import lax
from jax.experimental import pallas as pl
from jax.experimental.pallas import tpu as pltpu
from jax.sharding import PartitionSpec as P

BR = 8
MAXOFF = 2
MESH = pl.DeviceIdType.MESH
F32 = jnp.float32
BF16 = jnp.bfloat16


def build_bands(psf_ref, taps, size, bands):
    radius = size // 2
    half = 128
    for image in range(2):
        for part in range(2):
            bands[image, part, :, 0:half, half:] = jnp.zeros((size, half, half), BF16)
            bands[image, part, :, half:, 0:half] = jnp.zeros((size, half, half), BF16)

    def fill(a, carry):
        def place(rows, cols, shift, spots):
            diff = (
                lax.broadcasted_iota(jnp.int32, (rows, cols), 0)
                - lax.broadcasted_iota(jnp.int32, (rows, cols), 1)
                + shift
            )
            value = jnp.zeros((rows, cols), F32)
            for b in range(size):
                value = jnp.where(diff == b - radius, psf_ref[a, b], value)
            for image in range(2):
                full = value if image == 0 else value * value
                high = full.astype(BF16)
                low = (full - high.astype(F32)).astype(BF16)
                for row, col in spots:
                    bands[image, 0, a, row : row + rows, col : col + cols] = high
                    bands[image, 1, a, row : row + rows, col : col + cols] = low

        place(half, half, 0, ((0, 0), (half, half)))
        place(16, half, -16, ((half - 16, half),))
        place(16, half, half, ((half, 0),))
        return carry

    lax.fori_loop(0, size, fill, 0)


def kernel(
    sky_count,
    psf_ref,
    off_ref,
    sci_ref,
    inv_ref,
    out_ref,
    raw,
    high,
    low,
    bands,
    own,
    edge,
    part_send,
    part_own,
    part_recv,
    x_recv,
    raw_send_sem,
    raw_recv_sem,
    img_send_sem,
    img_recv_sem,
    core_send_sem,
    core_recv_sem,
    x_sems,
):
    visits, rows, cols = sci_ref.shape
    size = psf_ref.shape[0]
    radius = size // 2
    group = rows // 4
    gb, rb = group // BR, rows // BR
    sky = lax.axis_index("sky")
    me = lax.axis_index("visit")
    far, near = lax.div(me, 2), lax.rem(me, 2)
    mate = (sky, 2 * far + 1 - near)
    across = (sky, 2 * (1 - far) + near)
    above, below = (sky - 1, me), (sky + 1, me)
    has_above, has_below = sky > 0, sky < sky_count - 1

    barrier = pltpu.get_barrier_semaphore()
    pl.semaphore_signal(barrier, inc=1, device_id=mate, device_id_type=MESH)
    pl.semaphore_signal(barrier, inc=1, device_id=across, device_id_type=MESH)

    @pl.when(has_above)
    def _():
        pl.semaphore_signal(barrier, inc=1, device_id=above, device_id_type=MESH)

    @pl.when(has_below)
    def _():
        pl.semaphore_signal(barrier, inc=1, device_id=below, device_id_type=MESH)

    def turn(i, carry):
        at = pl.multiple_of(i * 8, 8)
        variance = inv_ref[:, pl.ds(at, 8), :]
        weighted = sci_ref[:, pl.ds(at, 8), :] * variance
        raw[0, pl.ds(radius + at, 8)] = jnp.swapaxes(weighted, 0, 1)
        raw[1, pl.ds(radius + at, 8)] = jnp.swapaxes(variance, 0, 1)
        return carry

    lax.fori_loop(0, rows // 8, turn, 0)

    pl.semaphore_wait(barrier, 2 + has_above.astype(jnp.int32) + has_below.astype(jnp.int32))

    def remote(src, dst, send_sem, recv_sem, device):
        return pltpu.make_async_remote_copy(
            src_ref=src,
            dst_ref=dst,
            send_sem=send_sem,
            recv_sem=recv_sem,
            device_id=device,
            device_id_type=MESH,
        )

    raw_up = remote(
        raw.at[:, radius : 2 * radius],
        raw.at[:, rows + radius : rows + 2 * radius],
        raw_send_sem.at[0],
        raw_recv_sem.at[0],
        above,
    )
    raw_down = remote(
        raw.at[:, rows : rows + radius],
        raw.at[:, 0:radius],
        raw_send_sem.at[1],
        raw_recv_sem.at[1],
        below,
    )

    @pl.when(has_above)
    def _():
        raw_up.start()

    @pl.when(has_below)
    def _():
        raw_down.start()

    @pl.when(jnp.logical_not(has_above))
    def _():
        raw[:, 0:radius] = jnp.zeros((2, radius, visits, cols), F32)
        edge[0, :, :, 0:MAXOFF] = jnp.zeros((2, visits, MAXOFF, BR, cols), F32)

    @pl.when(jnp.logical_not(has_below))
    def _():
        raw[:, rows + radius :] = jnp.zeros((2, radius, visits, cols), F32)
        edge[1, :, :, gb + MAXOFF :] = jnp.zeros((2, visits, MAXOFF, BR, cols), F32)

    build_bands(psf_ref, size, size, bands)

    @pl.when(has_above)
    def _():
        raw_down.wait_recv()

    @pl.when(has_below)
    def _():
        raw_up.wait_recv()

    def split(i, carry):
        for image in range(2):
            for odd in range(2):
                pair = raw[image, pl.ds(2 * i + odd, 2)].reshape(2 * visits, cols)
                first = pair.astype(BF16)
                high[image, odd, i] = first
                low[image, odd, i] = (pair - first.astype(F32)).astype(BF16)
        return carry

    pairs = (rows + 2 * radius) // 2
    lax.fori_loop(0, pairs - 1, split, 0)
    for image in range(2):
        pair = raw[image, rows + 2 * radius - 2 :].reshape(2 * visits, cols)
        first = pair.astype(BF16)
        high[image, 0, pairs - 1] = first
        low[image, 0, pairs - 1] = (pair - first.astype(F32)).astype(BF16)

    def correlate(image, starts, count):
        total = jnp.zeros((len(starts) * count * visits, cols), F32)
        for a in range(size):
            def rows_of(terms):
                pieces = [
                    terms[image, a % 2, (start + a) // 2 : (start + a) // 2 + count // 2].reshape(
                        count * visits, cols
                    )
                    for start in starts
                ]
                return pieces[0] if len(pieces) == 1 else jnp.concatenate(pieces, axis=0)

            x_high, x_low = rows_of(high), rows_of(low)
            w_high, w_low = bands[image, 0, a], bands[image, 1, a]
            total = total + jnp.dot(x_high, w_high, preferred_element_type=F32)
            total = total + jnp.dot(x_low, w_high, preferred_element_type=F32)
            total = total + jnp.dot(x_high, w_low, preferred_element_type=F32)
        turned = jnp.swapaxes(total.reshape(len(starts) * count, visits, cols), 0, 1)
        return turned.reshape(visits, len(starts) * count // BR, BR, cols)

    img_up = [
        remote(
            own.at[image, :, 0:MAXOFF],
            edge.at[1, image, :, gb + MAXOFF : gb + 2 * MAXOFF],
            img_send_sem.at[0, image],
            img_recv_sem.at[0, image],
            above,
        )
        for image in range(2)
    ]
    img_down = [
        remote(
            own.at[image, :, rb - MAXOFF : rb],
            edge.at[0, image, :, 0:MAXOFF],
            img_send_sem.at[1, image],
            img_recv_sem.at[1, image],
            below,
        )
        for image in range(2)
    ]

    for image in range(2):
        value = correlate(image, (0, rows - group), group)
        own[image, :, 0:gb] = value[:, 0:gb]
        own[image, :, rb - gb : rb] = value[:, gb:]
        edge[0, image, :, MAXOFF : MAXOFF + gb] = value[:, 0:gb]
        edge[1, image, :, MAXOFF : MAXOFF + gb] = value[:, gb:]

        @pl.when(has_above)
        def _():
            img_up[image].start()

        @pl.when(has_below)
        def _():
            img_down[image].start()

    for image in range(2):
        value = correlate(image, (group,), rows - 2 * group)
        own[image, :, gb : rb - gb] = value
        edge[0, image, :, MAXOFF + gb :] = value[:, 0:MAXOFF]
        edge[1, image, :, 0:MAXOFF] = value[:, rb - 2 * gb - MAXOFF :]

    def stack(load, base, target):
        def velocity(k, carry):
            totals = [[None] * gb, [None] * gb]
            for t in range(visits):
                first = base + off_ref[me * visits + t, k]
                for image in range(2):
                    for block in range(gb):
                        term = load(image, t, first + block)
                        held = totals[image][block]
                        totals[image][block] = term if held is None else held + term
            for image in range(2):
                for block in range(gb):
                    target[image, k, block] = totals[image][block]
            return carry

        lax.fori_loop(0, out_ref.shape[0], velocity, 0)

    def own_rows(image, t, block):
        return own[image, t, block]

    core = [
        remote(
            part_send.at[stage],
            part_recv.at[stage],
            core_send_sem.at[stage],
            core_recv_sem.at[stage],
            mate,
        )
        for stage in range(2)
    ]
    hop = [remote(part_own.at[stage], x_recv, x_sems.at[0], x_sems.at[1], across) for stage in range(2)]

    def gather(stage):
        def add(k, carry):
            for image in range(2):
                part_own[stage, image, k] += part_recv[stage, image, k]
            return carry

        lax.fori_loop(0, out_ref.shape[0], add, 0)

    stack(own_rows, (1 + near) * gb, part_send.at[0])
    core[0].start()
    stack(own_rows, (2 - near) * gb, part_own.at[0])
    core[0].wait_recv()
    gather(0)

    @pl.when(far == near)
    def _():
        hop[0].start()

    for image in range(2):

        @pl.when(has_above)
        def _():
            img_down[image].wait_recv()

        @pl.when(has_below)
        def _():
            img_up[image].wait_recv()

    stack(lambda image, t, block: edge[1 - near, image, t, block], MAXOFF, part_send.at[1])
    core[1].start()
    stack(lambda image, t, block: edge[near, image, t, block], MAXOFF, part_own.at[1])
    core[1].wait_recv()
    gather(1)

    @pl.when(far != near)
    def _():
        hop[1].start()

    hop[0].wait_recv()

    def finish(stage):
        def velocity(k, carry):
            top = part_own[stage, 0, k] + x_recv[0, k]
            bottom = part_own[stage, 1, k] + x_recv[1, k]
            out_ref[k] = (top / jnp.sqrt(bottom)).reshape(group, cols)
            return carry

        lax.fori_loop(0, out_ref.shape[0], velocity, 0)

    @pl.when(far == near)
    def _():
        finish(1)

    @pl.when(far != near)
    def _():
        finish(0)

    @pl.when(has_above)
    def _():
        raw_up.wait_send()
        img_up[0].wait_send()
        img_up[1].wait_send()

    @pl.when(has_below)
    def _():
        raw_down.wait_send()
        img_down[0].wait_send()
        img_down[1].wait_send()

    core[0].wait_send()
    core[1].wait_send()
    hop[0].wait_send()


def solution(mesh):
    sky_count = mesh.shape["sky"]

    def shards(science, inv_variance, psf_kernel, offsets):
        visits, rows, cols = science.shape
        size = psf_kernel.shape[0]
        velocities = offsets.shape[1]
        radius, group = size // 2, rows // 4
        depth = rows + 2 * radius
        vmem = pl.BlockSpec(memory_space=pltpu.VMEM)
        smem = pl.BlockSpec(memory_space=pltpu.SMEM)
        parts = (2, 2, velocities, group // BR, BR, cols)
        dma = pltpu.SemaphoreType.DMA

        def body(*refs):
            kernel(sky_count, *refs)

        return pl.pallas_call(
            body,
            out_shape=jax.ShapeDtypeStruct((velocities, group, cols), F32),
            in_specs=[smem, smem, vmem, vmem],
            out_specs=vmem,
            scratch_shapes=[
                pltpu.VMEM((2, depth, visits, cols), F32),
                pltpu.VMEM((2, 2, depth // 2, 2 * visits, cols), BF16),
                pltpu.VMEM((2, 2, depth // 2, 2 * visits, cols), BF16),
                pltpu.VMEM((2, 2, size, cols, cols), BF16),
                pltpu.VMEM((2, visits, rows // BR, BR, cols), F32),
                pltpu.VMEM((2, 2, visits, group // BR + 2 * MAXOFF, BR, cols), F32),
                pltpu.VMEM(parts, F32),
                pltpu.VMEM(parts, F32),
                pltpu.VMEM(parts, F32),
                pltpu.VMEM(parts[1:], F32),
                dma((2,)),
                dma((2,)),
                dma((2, 2)),
                dma((2, 2)),
                dma((2,)),
                dma((2,)),
                dma((2,)),
            ],
            compiler_params=pltpu.CompilerParams(
                collective_id=0, has_side_effects=True, vmem_limit_bytes=48 * 1024 * 1024
            ),
        )(psf_kernel, offsets, science, inv_variance)

    return jax.shard_map(
        shards,
        mesh=mesh,
        in_specs=(P("visit", "sky", None), P("visit", "sky", None), P(), P()),
        out_specs=P(None, ("sky", "visit"), None),
        check_vma=False,
    )
```

time: 90.5 us -> 37.7 us (0.42)
  the two profiles are of different devices: /device:TPU:1 before, /device:TPU:20 now
where the time goes in v1:
time: 37.7 us; the launch traced here: 37.4 us
  Pallas kernels  33.8 us (90%)
  local copies, waits for them, and re-layouts  3.58 us (9%)
    pallas_call x1, Pallas kernels, shards(): pl.pallas_call(body, out_shape=jax.ShapeDtypeStruct((velocities, group, c...  33.8 us
    unnamed x8, local copies, waits for them, and re-layouts  3.58 us

profile of v1, /device:TPU:20, one launch (start us, length us, event | category | flops | bytes accessed | tf_op | source)
XLA Modules:
  0.0 37.4 jit_solution(7664920941257529721)
XLA Ops:
  0.0 0.0 copy-start.2
  0.0 0.8 %copy.5.refs_1_ = s32[32,16]{1,0:T(8,128)S(1)} copy(s32[32,16]{0,1:T(8,128)} %param.7) | data formatting | bytes 4096 | tf_op args[3]
  0.8 0.0 copy-done.2
  0.8 0.0 copy-start
  0.8 1.0 %copy-done = f32[8,64,256]{2,1,0:T(8,128)S(1)} copy-done((f32[8,64,256]{2,1,0:T(8,128)S(1)}, f32[8,64,256]{2,1,0:T(8,128)}, u32[]{:S(2)}) %copy-start) | copy-done | bytes 524312
  1.8 0.0 copy-start.1
  1.8 1.0 %copy-done.1 = f32[8,64,256]{2,1,0:T(8,128)S(1)} copy-done((f32[8,64,256]{2,1,0:T(8,128)S(1)}, f32[8,64,256]{2,1,0:T(8,128)}, u32[]{:S(2)}) %copy-start.1) | copy-done | bytes 524312
  2.9 33.8 %shard_map.46 = f32[16,16,256]{2,1,0:T(8,128)S(1)} custom-call(f32[11,11]{1,0:T(8,128)S(1)} %copy-done.2, s32[32,16]{1,0:T(8,128)S(1)} %copy.5.refs_1_, f32[8,64,256]{2,1,0:T(8,128)S(1)} %copy-done, f32[8,64,256]{2,1,0:T(8,128)S(1)} %copy-done.1), custom_call_target="tpu_custom_call" | custom-call | tf_op jit(solution)/shard_map/pallas_call | solution.py:366
  36.7 0.7 %copy.7 = f32[16,16,256]{2,1,0:T(8,128)} copy(f32[16,16,256]{2,1,0:T(8,128)S(1)} %shard_map.46) | data formatting | bytes 524288
Async XLA Ops:
  0.0 0.8 %copy-start.2 = (f32[11,11]{1,0:T(8,128)S(1)}, f32[11,11]{1,0:T(8,128)}, u32[]{:S(2)}) copy-start(f32[11,11]{1,0:T(8,128)} %refs_0_.1) | copy-start | bytes 1456
  0.8 1.0 %copy-start = (f32[8,64,256]{2,1,0:T(8,128)S(1)}, f32[8,64,256]{2,1,0:T(8,128)}, u32[]{:S(2)}) copy-start(f32[8,64,256]{2,1,0:T(8,128)} %refs_2_.1) | copy-start | bytes 1572868
  1.8 1.0 %copy-start.1 = (f32[8,64,256]{2,1,0:T(8,128)S(1)}, f32[8,64,256]{2,1,0:T(8,128)}, u32[]{:S(2)}) copy-start(f32[8,64,256]{2,1,0:T(8,128)} %refs_3_.1) | copy-start | bytes 1572868

commit v2 on v0

v2 whole, which is shorter than its diff:
```python
import jax
import jax.numpy as jnp
from jax import lax
from jax.experimental import pallas as pl
from jax.experimental.pallas import tpu as pltpu
from jax.sharding import PartitionSpec as P

BR = 8
MAXOFF = 2
MESH = pl.DeviceIdType.MESH
F32 = jnp.float32
BF16 = jnp.bfloat16


def build_bands(psf_ref, taps, size, bands):
    radius = size // 2
    half = 128
    for image in range(2):
        for part in range(2):
            bands[image, part, :, 0:half, half:] = jnp.zeros((size, half, half), BF16)
            bands[image, part, :, half:, 0:half] = jnp.zeros((size, half, half), BF16)

    def fill(a, carry):
        def place(rows, cols, shift, spots):
            diff = (
                lax.broadcasted_iota(jnp.int32, (rows, cols), 0)
                - lax.broadcasted_iota(jnp.int32, (rows, cols), 1)
                + shift
            )
            value = jnp.zeros((rows, cols), F32)
            for b in range(size):
                value = jnp.where(diff == b - radius, psf_ref[a, b], value)
            for image in range(2):
                full = value if image == 0 else value * value
                high = full.astype(BF16)
                low = (full - high.astype(F32)).astype(BF16)
                for row, col in spots:
                    bands[image, 0, a, row : row + rows, col : col + cols] = high
                    bands[image, 1, a, row : row + rows, col : col + cols] = low

        place(half, half, 0, ((0, 0), (half, half)))
        place(16, half, -16, ((half - 16, half),))
        place(16, half, half, ((half, 0),))
        return carry

    lax.fori_loop(0, size, fill, 0)


def kernel(
    sky_count,
    psf_ref,
    off_ref,
    sci_hbm,
    inv_hbm,
    out_ref,
    sci_ref,
    inv_ref,
    raw,
    high,
    low,
    bands,
    images,
    part_send,
    part_own,
    part_recv,
    x_recv,
    load_sems,
    raw_send_sem,
    raw_recv_sem,
    core_send_sem,
    core_recv_sem,
    x_send_sem,
    x_recv_sem,
):
    visits, rows, cols = sci_ref.shape
    size = psf_ref.shape[0]
    radius = size // 2
    halo = radius + MAXOFF * BR
    blocks = rows // BR
    velocities = off_ref.shape[0]
    sky = lax.axis_index("sky")
    me = lax.axis_index("visit")
    far, near = lax.div(me, 2), lax.rem(me, 2)
    mate = (sky, 2 * far + 1 - near)
    across = (sky, 2 * (1 - far) + near)
    above, below = (sky - 1, me), (sky + 1, me)
    has_above, has_below = sky > 0, sky < sky_count - 1

    load_sci = pltpu.make_async_copy(sci_hbm, sci_ref, load_sems.at[0])
    load_inv = pltpu.make_async_copy(inv_hbm, inv_ref, load_sems.at[1])
    load_sci.start()
    load_inv.start()

    barrier = pltpu.get_barrier_semaphore()
    pl.semaphore_signal(barrier, inc=1, device_id=mate, device_id_type=MESH)
    pl.semaphore_signal(barrier, inc=1, device_id=across, device_id_type=MESH)

    @pl.when(has_above)
    def _():
        pl.semaphore_signal(barrier, inc=1, device_id=above, device_id_type=MESH)

    @pl.when(has_below)
    def _():
        pl.semaphore_signal(barrier, inc=1, device_id=below, device_id_type=MESH)

    def turn(first, count):
        def block(i, carry):
            at = pl.multiple_of(i * BR, BR)
            variance = inv_ref[:, pl.ds(at, BR), :]
            weighted = sci_ref[:, pl.ds(at, BR), :] * variance
            raw[0, pl.ds(halo + at, BR)] = jnp.swapaxes(weighted, 0, 1)
            raw[1, pl.ds(halo + at, BR)] = jnp.swapaxes(variance, 0, 1)
            return carry

        lax.fori_loop(first, first + count, block, 0)

    def remote(src, dst, send_sem, recv_sem, device):
        return pltpu.make_async_remote_copy(
            src_ref=src,
            dst_ref=dst,
            send_sem=send_sem,
            recv_sem=recv_sem,
            device_id=device,
            device_id_type=MESH,
        )

    def raw_copy(way, chunk, source, target, count, device):
        return remote(
            raw.at[:, source : source + count],
            raw.at[:, target : target + count],
            raw_send_sem.at[way, chunk],
            raw_recv_sem.at[way, chunk],
            device,
        )

    inner = halo - BR
    up = [
        raw_copy(0, 0, halo, halo + rows, inner, above),
        raw_copy(0, 1, halo + inner, halo + rows + inner, BR, above),
    ]
    down = [
        raw_copy(1, 0, halo + rows - inner, BR, inner, below),
        raw_copy(1, 1, rows, 0, BR, below),
    ]
    edge_blocks = (halo + BR - 1) // BR

    load_sci.wait()
    load_inv.wait()
    turn(0, edge_blocks)
    turn(blocks - edge_blocks, edge_blocks)
    pl.semaphore_wait(barrier, 2 + has_above.astype(jnp.int32) + has_below.astype(jnp.int32))

    for chunk in range(2):

        @pl.when(has_above)
        def _():
            up[chunk].start()

        @pl.when(has_below)
        def _():
            down[chunk].start()

    @pl.when(jnp.logical_not(has_above))
    def _():
        raw[:, 0:halo] = jnp.zeros((2, halo, visits, cols), F32)

    @pl.when(jnp.logical_not(has_below))
    def _():
        raw[:, halo + rows :] = jnp.zeros((2, halo, visits, cols), F32)

    turn(edge_blocks, blocks - 2 * edge_blocks)
    build_bands(psf_ref, size, size, bands)

    def split(odd, first, last):
        def pair_of(i, carry):
            for image in range(2):
                pair = raw[image, pl.ds(2 * i + odd, 2)].reshape(2 * visits, cols)
                head = pair.astype(BF16)
                high[image, odd, i] = head
                low[image, odd, i] = (pair - head.astype(F32)).astype(BF16)
            return carry

        lax.fori_loop(first, last, pair_of, 0)

    def correlate(starts, count):
        def image_of(image, carry):
            total = jnp.zeros((len(starts) * count * visits, cols), F32)
            for a in range(size):

                def rows_of(terms):
                    pieces = [
                        terms[image, a % 2, (start + a) // 2 : (start + a) // 2 + count // 2].reshape(
                            count * visits, cols
                        )
                        for start in starts
                    ]
                    return pieces[0] if len(pieces) == 1 else jnp.concatenate(pieces, axis=0)

                x_high, x_low = rows_of(high), rows_of(low)
                w_high, w_low = bands[image, 0, a], bands[image, 1, a]
                total = total + jnp.dot(x_high, w_high, preferred_element_type=F32)
                total = total + jnp.dot(x_low, w_high, preferred_element_type=F32)
                total = total + jnp.dot(x_high, w_low, preferred_element_type=F32)
            value = jnp.swapaxes(total.reshape(len(starts) * count, visits, cols), 0, 1)
            value = value.reshape(visits, len(starts) * count // BR, BR, cols)
            many = count // BR
            for i, start in enumerate(starts):
                images[image, :, start // BR : start // BR + many] = value[:, i * many : (i + 1) * many]
            return carry

        lax.fori_loop(0, 2, image_of, 0)

    def stack(block, target):
        def velocity(k, carry):
            totals = [None, None]
            for t in range(visits):
                place = block + MAXOFF + off_ref[k, me * visits + t]
                for image in range(2):
                    term = images[image, t, place]
                    totals[image] = term if t == 0 else totals[image] + term
            target[0, k] = totals[0]
            target[1, k] = totals[1]
            return carry

        lax.fori_loop(0, velocities, velocity, 0)

    core = [
        remote(
            part_send.at[stage],
            part_recv.at[stage],
            core_send_sem.at[stage],
            core_recv_sem.at[stage],
            mate,
        )
        for stage in range(4)
    ]
    hop = [
        remote(
            part_own.at[stage],
            x_recv.at[stage % 2],
            x_send_sem.at[stage % 2],
            x_recv_sem.at[stage % 2],
            across,
        )
        for stage in range(4)
    ]
    middle, last = blocks // 2, blocks - 1
    mine = [
        middle - near,
        middle + 1 - 3 * near,
        1 + (last - 2) * near,
        last * near,
    ]
    other = [last - block for block in mine]
    early_goes = far == near

    def give(stage):
        stack(other[stage], part_send.at[stage])
        core[stage].start()

    def keep(stage):
        stack(mine[stage], part_own.at[stage])

    def gather(stage):
        core[stage].wait_recv()

        def add(k, carry):
            for image in range(2):
                part_own[stage, image, k] += part_recv[stage, image, k]
            return carry

        lax.fori_loop(0, velocities, add, 0)

        @pl.when(early_goes if stage < 2 else jnp.logical_not(early_goes))
        def _():
            hop[stage].start()

    def arrived(chunk):
        @pl.when(has_above)
        def _():
            down[chunk].wait_recv()

        @pl.when(has_below)
        def _():
            up[chunk].wait_recv()

    def outside(block):
        @pl.when(jnp.logical_not(has_above))
        def _():
            images[:, :, block] = jnp.zeros((2, visits, BR, cols), F32)

        @pl.when(jnp.logical_not(has_below))
        def _():
            images[:, :, blocks + 2 * MAXOFF - 1 - block] = jnp.zeros((2, visits, BR, cols), F32)

    depth = rows + 2 * halo
    total_blocks = blocks + 2 * MAXOFF
    lead = 3 * BR
    lo, hi = lead // 2, (depth - lead) // 2
    split(0, lo, hi)
    split(1, lo, hi)
    correlate((lead,), rows + 2 * MAXOFF * BR - 2 * lead)
    give(0)
    keep(0)
    gather(0)

    arrived(0)
    lo1, hi1 = BR // 2, (depth - BR) // 2
    split(0, lo1, lo)
    split(1, lo1, lo)
    split(0, hi, hi1)
    split(1, hi, hi1 - 1)
    correlate((BR, (total_blocks - 3) * BR), 2 * BR)
    outside(1)
    give(1)
    give(2)
    keep(1)
    gather(1)
    keep(2)
    gather(2)

    arrived(1)
    split(0, 0, lo1)
    split(1, 0, lo1)
    split(0, hi1, depth // 2)
    split(1, hi1 - 1, depth // 2 - 1)
    correlate((0, (total_blocks - 1) * BR), BR)
    outside(0)
    give(3)
    keep(3)
    gather(3)

    def finish(stage, place):
        hop[stage].wait_recv()

        def velocity(k, carry):
            top = part_own[stage, 0, k] + x_recv[stage % 2, 0, k]
            bottom = part_own[stage, 1, k] + x_recv[stage % 2, 1, k]
            out_ref[k, place] = top / jnp.sqrt(bottom)
            return carry

        lax.fori_loop(0, velocities, velocity, 0)

    @pl.when(early_goes)
    def _():
        finish(2, 1 - near)
        finish(3, near)

    @pl.when(jnp.logical_not(early_goes))
    def _():
        finish(0, near)
        finish(1, 1 - near)

    for chunk in range(2):

        @pl.when(has_above)
        def _():
            up[chunk].wait_send()

        @pl.when(has_below)
        def _():
            down[chunk].wait_send()

    for stage in range(4):
        core[stage].wait_send()
    hop[0].wait_send()
    hop[1].wait_send()


def solution(mesh):
    sky_count = mesh.shape["sky"]

    def shards(science, inv_variance, psf_kernel, offsets):
        visits, rows, cols = science.shape
        size = psf_kernel.shape[0]
        velocities = offsets.shape[1]
        group = rows // 4
        depth = rows + 2 * (size // 2 + MAXOFF * BR)
        hbm = pl.BlockSpec(memory_space=pltpu.HBM)
        vmem = pl.BlockSpec(memory_space=pltpu.VMEM)
        smem = pl.BlockSpec(memory_space=pltpu.SMEM)
        parts = (4, 2, velocities, BR, cols)
        dma = pltpu.SemaphoreType.DMA

        def body(*refs):
            kernel(sky_count, *refs)

        stacked = pl.pallas_call(
            body,
            out_shape=jax.ShapeDtypeStruct((velocities, group // BR, BR, cols), F32),
            in_specs=[smem, smem, hbm, hbm],
            out_specs=vmem,
            scratch_shapes=[
                pltpu.VMEM((visits, rows, cols), F32),
                pltpu.VMEM((visits, rows, cols), F32),
                pltpu.VMEM((2, depth, visits, cols), F32),
                pltpu.VMEM((2, 2, depth // 2, 2 * visits, cols), BF16),
                pltpu.VMEM((2, 2, depth // 2, 2 * visits, cols), BF16),
                pltpu.VMEM((2, 2, size, cols, cols), BF16),
                pltpu.VMEM((2, visits, rows // BR + 2 * MAXOFF, BR, cols), F32),
                pltpu.VMEM(parts, F32),
                pltpu.VMEM(parts, F32),
                pltpu.VMEM(parts, F32),
                pltpu.VMEM((2,) + parts[1:], F32),
                dma((2,)),
                dma((2, 2)),
                dma((2, 2)),
                dma((4,)),
                dma((4,)),
                dma((2,)),
                dma((2,)),
            ],
            compiler_params=pltpu.CompilerParams(
                collective_id=0, has_side_effects=True, vmem_limit_bytes=48 * 1024 * 1024
            ),
        )(psf_kernel, offsets.T, science, inv_variance)
        return stacked.reshape(velocities, group, cols)

    return jax.shard_map(
        shards,
        mesh=mesh,
        in_specs=(P("visit", "sky", None), P("visit", "sky", None), P(), P()),
        out_specs=P(None, ("sky", "visit"), None),
        check_vma=False,
    )
```

time: 90.5 us -> 37 us (0.41)
  the two profiles are of different devices: /device:TPU:1 before, /device:TPU:24 now
where the time goes in v2:
time: 37 us; the launch traced here: 36.5 us
  Pallas kernels  32.3 us (87%)
  local copies, waits for them, and re-layouts  4.18 us (11%)
    pallas_call x1, Pallas kernels, shards(): pl.pallas_call(body, out_shape=jax.ShapeDtypeStruct((velocities, group //...  32.3 us
    unnamed x9, local copies, waits for them, and re-layouts  4.18 us

profile of v2, /device:TPU:24, one launch (start us, length us, event | category | flops | bytes accessed | tf_op | source)
XLA Modules:
  0.0 36.5 jit_solution(8352915974030365774)
XLA Ops:
  0.0 0.0 copy-start
  0.0 1.0 %copy-done = f32[8,64,256]{2,1,0:T(8,128)S(1)} copy-done((f32[8,64,256]{2,1,0:T(8,128)S(1)}, f32[8,64,256]{2,1,0:T(8,128)}, u32[]{:S(2)}) %copy-start) | copy-done | bytes 524312
  1.0 0.0 copy-start.1
  1.0 1.0 %copy-done.1 = f32[8,64,256]{2,1,0:T(8,128)S(1)} copy-done((f32[8,64,256]{2,1,0:T(8,128)S(1)}, f32[8,64,256]{2,1,0:T(8,128)}, u32[]{:S(2)}) %copy-start.1) | copy-done | bytes 524312
  2.1 0.0 copy-start.2
  2.1 0.7 %copy-done.2 = f32[11,11]{1,0:T(8,128)S(1)} copy-done((f32[11,11]{1,0:T(8,128)S(1)}, f32[11,11]{1,0:T(8,128)}, u32[]{:S(2)}) %copy-start.2) | copy-done | bytes 508
  2.8 0.0 copy-start.3
  2.8 0.7 %copy-done.3 = s32[32,16]{0,1:T(8,128)S(1)} copy-done((s32[32,16]{0,1:T(8,128)S(1)}, s32[32,16]{0,1:T(8,128)}, u32[]{:S(2)}) %copy-start.3) | copy-done | bytes 2072
  3.5 32.3 %shard_map.46 = f32[16,2,8,256]{3,2,1,0:T(8,128)S(1)} custom-call(f32[11,11]{1,0:T(8,128)S(1)} %copy-done.2, s32[16,32]{1,0:T(8,128)S(1)} %bitcast.3, f32[8,64,256]{2,1,0:T(8,128)S(1)} %copy-done, f32[8,64,256]{2,1,0:T(8,128)S(1)} %copy-done.1), custom_call_target="tpu_custom_call" | custom-call | tf_op jit(solution)/shard_map/pallas_call | solution.py:388
  35.8 0.7 %copy.6 = f32[16,16,256]{2,1,0:T(8,128)} copy(f32[16,16,256]{2,1,0:T(8,128)S(1)} %bitcast.2) | data formatting | bytes 524288
Async XLA Ops:
  0.0 1.0 %copy-start = (f32[8,64,256]{2,1,0:T(8,128)S(1)}, f32[8,64,256]{2,1,0:T(8,128)}, u32[]{:S(2)}) copy-start(f32[8,64,256]{2,1,0:T(8,128)} %refs_2_.1) | copy-start | bytes 1572868
  1.0 1.0 %copy-start.1 = (f32[8,64,256]{2,1,0:T(8,128)S(1)}, f32[8,64,256]{2,1,0:T(8,128)}, u32[]{:S(2)}) copy-start(f32[8,64,256]{2,1,0:T(8,128)} %refs_3_.1) | copy-start | bytes 1572868
  2.1 0.7 %copy-start.2 = (f32[11,11]{1,0:T(8,128)S(1)}, f32[11,11]{1,0:T(8,128)}, u32[]{:S(2)}) copy-start(f32[11,11]{1,0:T(8,128)} %refs_0_.1) | copy-start | bytes 1456
  2.8 0.7 %copy-start.3 = (s32[32,16]{0,1:T(8,128)S(1)}, s32[32,16]{0,1:T(8,128)}, u32[]{:S(2)}) copy-start(s32[32,16]{0,1:T(8,128)} %param.7) | copy-start | bytes 6148

commit v3 on v2

--- a/solution.py
+++ b/solution.py
@@ -411,7 +411,7 @@
                 dma((2,)),
             ],
             compiler_params=pltpu.CompilerParams(
-                collective_id=0, has_side_effects=True, vmem_limit_bytes=48 * 1024 * 1024
+                collective_id=0, has_side_effects=True, vmem_limit_bytes=63 * 1024 * 1024
             ),
         )(psf_kernel, offsets.T, science, inv_variance)
         return stacked.reshape(velocities, group, cols)

time: 37 us -> 35.2 us (0.951)
  local copies, waits for them, and re-layouts: 4.18 us -> 1.67 us
  Pallas kernels: 32.3 us -> 33.2 us
    unnamed x9 -> x1, local copies, waits for them, and re-layouts: 4.18 us -> 1.67 us
    pallas_call x1, Pallas kernels: 32.3 us -> 33.2 us  [shards(): pl.pallas_call(body, out_shape=jax.ShapeDtypeStruct((velocities, group //...]
where the time goes in v3:
time: 35.2 us; the launch traced here: 34.9 us
  Pallas kernels  33.2 us (94%)
  local copies, waits for them, and re-layouts  1.67 us (5%)
    pallas_call x1, Pallas kernels, shards(): pl.pallas_call(body, out_shape=jax.ShapeDtypeStruct((velocities, group //...  33.2 us
    unnamed x1, local copies, waits for them, and re-layouts  1.67 us

profile of v3, /device:TPU:24, one launch (start us, length us, event | category | flops | bytes accessed | tf_op | source)
XLA Modules:
  0.0 34.9 jit_solution(13668383232774088229)
XLA Ops:
  0.0 33.2 %shard_map.46 = f32[16,2,8,256]{3,2,1,0:T(8,128)} custom-call(f32[11,11]{1,0:T(8,128)} %refs_0_.1, s32[16,32]{1,0:T(8,128)} %bitcast.3, f32[8,64,256]{2,1,0:T(8,128)} %refs_2_.1, f32[8,64,256]{2,1,0:T(8,128)} %refs_3_.1), custom_call_target="tpu_custom_call" | custom-call | tf_op jit(solution)/shard_map/pallas_call | solution.py:388
  33.2 1.7 %copy.6 = f32[16,16,256]{2,1,0:T(8,128)} copy(f32[16,16,256]{2,1,0:T(8,128)} %bitcast.2) | data formatting | bytes 524288

commit v4 on v3

--- a/solution.py
+++ b/solution.py
@@ -60,6 +60,7 @@
     low,
     bands,
     images,
+    outer,
     part_send,
     part_own,
     part_recv,
@@ -75,7 +76,7 @@
     visits, rows, cols = sci_ref.shape
     size = psf_ref.shape[0]
     radius = size // 2
-    halo = radius + MAXOFF * BR
+    halo = radius + BR
     blocks = rows // BR
     velocities = off_ref.shape[0]
     sky = lax.axis_index("sky")
@@ -124,25 +125,48 @@
             device_id_type=MESH,
         )
 
-    def raw_copy(way, chunk, source, target, count, device):
-        return remote(
-            raw.at[:, source : source + count],
-            raw.at[:, target : target + count],
-            raw_send_sem.at[way, chunk],
-            raw_recv_sem.at[way, chunk],
-            device,
-        )
-
-    inner = halo - BR
     up = [
-        raw_copy(0, 0, halo, halo + rows, inner, above),
-        raw_copy(0, 1, halo + inner, halo + rows + inner, BR, above),
+        remote(
+            raw.at[:, halo : 2 * halo],
+            raw.at[:, halo + rows :],
+            raw_send_sem.at[0, 0],
+            raw_recv_sem.at[0, 0],
+            above,
+        ),
+        remote(
+            images.at[:, :, MAXOFF + 1],
+            outer.at[1],
+            raw_send_sem.at[0, 1],
+            raw_recv_sem.at[0, 1],
+            above,
+        ),
     ]
     down = [
-        raw_copy(1, 0, halo + rows - inner, BR, inner, below),
-        raw_copy(1, 1, rows, 0, BR, below),
+        remote(
+            raw.at[:, rows : rows + halo],
+            raw.at[:, 0:halo],
+            raw_send_sem.at[1, 0],
+            raw_recv_sem.at[1, 0],
+            below,
+        ),
+        remote(
+            images.at[:, :, MAXOFF + blocks - 2],
+            outer.at[0],
+            raw_send_sem.at[1, 1],
+            raw_recv_sem.at[1, 1],
+            below,
+        ),
     ]
     edge_blocks = (halo + BR - 1) // BR
+
+    def depart(chunk):
+        @pl.when(has_above)
+        def _():
+            up[chunk].start()
+
+        @pl.when(has_below)
+        def _():
+            down[chunk].start()
 
     load_sci.wait()
     load_inv.wait()
@@ -150,15 +174,7 @@
     turn(blocks - edge_blocks, edge_blocks)
     pl.semaphore_wait(barrier, 2 + has_above.astype(jnp.int32) + has_below.astype(jnp.int32))
 
-    for chunk in range(2):
-
-        @pl.when(has_above)
-        def _():
-            up[chunk].start()
-
-        @pl.when(has_below)
-        def _():
-            down[chunk].start()
+    depart(0)
 
     @pl.when(jnp.logical_not(has_above))
     def _():
@@ -205,7 +221,7 @@
             value = value.reshape(visits, len(starts) * count // BR, BR, cols)
             many = count // BR
             for i, start in enumerate(starts):
-                images[image, :, start // BR : start // BR + many] = value[:, i * many : (i + 1) * many]
+                images[image, :, 1 + start // BR : 1 + start // BR + many] = value[:, i * many : (i + 1) * many]
             return carry
 
         lax.fori_loop(0, 2, image_of, 0)
@@ -294,23 +310,22 @@
             images[:, :, blocks + 2 * MAXOFF - 1 - block] = jnp.zeros((2, visits, BR, cols), F32)
 
     depth = rows + 2 * halo
-    total_blocks = blocks + 2 * MAXOFF
-    lead = 3 * BR
+    lead = 2 * BR
     lo, hi = lead // 2, (depth - lead) // 2
     split(0, lo, hi)
     split(1, lo, hi)
-    correlate((lead,), rows + 2 * MAXOFF * BR - 2 * lead)
+    correlate((lead,), rows + 2 * BR - 2 * lead)
+    depart(1)
     give(0)
     keep(0)
     gather(0)
 
     arrived(0)
-    lo1, hi1 = BR // 2, (depth - BR) // 2
-    split(0, lo1, lo)
-    split(1, lo1, lo)
-    split(0, hi, hi1)
-    split(1, hi, hi1 - 1)
-    correlate((BR, (total_blocks - 3) * BR), 2 * BR)
+    split(0, 0, lo)
+    split(1, 0, lo)
+    split(0, hi, depth // 2)
+    split(1, hi, depth // 2 - 1)
+    correlate((0, rows), lead)
     outside(1)
     give(1)
     give(2)
@@ -320,11 +335,15 @@
     gather(2)
 
     arrived(1)
-    split(0, 0, lo1)
-    split(1, 0, lo1)
-    split(0, hi1, depth // 2)
-    split(1, hi1 - 1, depth // 2 - 1)
-    correlate((0, (total_blocks - 1) * BR), BR)
+
+    @pl.when(has_above)
+    def _():
+        images[:, :, 0] = outer[0]
+
+    @pl.when(has_below)
+    def _():
+        images[:, :, blocks + 2 * MAXOFF - 1] = outer[1]
+
     outside(0)
     give(3)
     keep(3)
@@ -375,7 +394,7 @@
         size = psf_kernel.shape[0]
         velocities = offsets.shape[1]
         group = rows // 4
-        depth = rows + 2 * (size // 2 + MAXOFF * BR)
+        depth = rows + 2 * (size // 2 + BR)
         hbm = pl.BlockSpec(memory_space=pltpu.HBM)
         vmem = pl.BlockSpec(memory_space=pltpu.VMEM)
         smem = pl.BlockSpec(memory_space=pltpu.SMEM)
@@ -398,6 +417,7 @@
                 pltpu.VMEM((2, 2, depth // 2, 2 * visits, cols), BF16),
                 pltpu.VMEM((2, 2, size, cols, cols), BF16),
                 pltpu.VMEM((2, visits, rows // BR + 2 * MAXOFF, BR, cols), F32),
+                pltpu.VMEM((2, 2, visits, BR, cols), F32),
                 pltpu.VMEM(parts, F32),
                 pltpu.VMEM(parts, F32),
                 pltpu.VMEM(parts, F32),

time: 35.2 us -> 35.2 us (level)
  no operation moved by 1% of the time
where the time goes in v4:
time: 35.2 us; the launch traced here: 34.8 us
  Pallas kernels  33.2 us (94%)
  local copies, waits for them, and re-layouts  1.67 us (5%)
    pallas_call x1, Pallas kernels, shards(): pl.pallas_call(body, out_shape=jax.ShapeDtypeStruct((velocities, group //...  33.2 us
    unnamed x1, local copies, waits for them, and re-layouts  1.67 us

profile of v4, /device:TPU:24, one launch (start us, length us, event | category | flops | bytes accessed | tf_op | source)
XLA Modules:
  0.0 34.8 jit_solution(6116494646209181794)
XLA Ops:
  0.0 33.2 %shard_map.46 = f32[16,2,8,256]{3,2,1,0:T(8,128)} custom-call(f32[11,11]{1,0:T(8,128)} %refs_0_.1, s32[16,32]{1,0:T(8,128)} %bitcast.3, f32[8,64,256]{2,1,0:T(8,128)} %refs_2_.1, f32[8,64,256]{2,1,0:T(8,128)} %refs_3_.1), custom_call_target="tpu_custom_call" | custom-call | tf_op jit(solution)/shard_map/pallas_call | solution.py:407
  33.2 1.7 %copy.6 = f32[16,16,256]{2,1,0:T(8,128)} copy(f32[16,16,256]{2,1,0:T(8,128)} %bitcast.2) | data formatting | bytes 524288

commit v5 on v4

--- a/solution.py
+++ b/solution.py
@@ -188,15 +188,24 @@
     build_bands(psf_ref, size, size, bands)
 
     def split(odd, first, last):
-        def pair_of(i, carry):
+        def pairs_of(first, count):
             for image in range(2):
-                pair = raw[image, pl.ds(2 * i + odd, 2)].reshape(2 * visits, cols)
-                head = pair.astype(BF16)
-                high[image, odd, i] = head
-                low[image, odd, i] = (pair - head.astype(F32)).astype(BF16)
-            return carry
-
-        lax.fori_loop(first, last, pair_of, 0)
+                rows_in = raw[image, pl.ds(2 * first + odd, 2 * count)]
+                pairs = rows_in.reshape(count, 2 * visits, cols)
+                head = pairs.astype(BF16)
+                high[image, odd, pl.ds(first, count)] = head
+                low[image, odd, pl.ds(first, count)] = (pairs - head.astype(F32)).astype(BF16)
+
+        step = 4
+
+        def several(i, carry):
+            pairs_of(first + step * i, step)
+            return carry
+
+        steps = (last - first) // step
+        lax.fori_loop(0, steps, several, 0)
+        if first + step * steps < last:
+            pairs_of(first + step * steps, last - first - step * steps)
 
     def correlate(starts, count):
         def image_of(image, carry):
@@ -238,7 +247,7 @@
             target[1, k] = totals[1]
             return carry
 
-        lax.fori_loop(0, velocities, velocity, 0)
+        lax.fori_loop(0, velocities, velocity, 0, unroll=4)
 
     core = [
         remote(
@@ -285,7 +294,7 @@
                 part_own[stage, image, k] += part_recv[stage, image, k]
             return carry
 
-        lax.fori_loop(0, velocities, add, 0)
+        lax.fori_loop(0, velocities, add, 0, unroll=4)
 
         @pl.when(early_goes if stage < 2 else jnp.logical_not(early_goes))
         def _():
@@ -318,7 +327,6 @@
     depart(1)
     give(0)
     keep(0)
-    gather(0)
 
     arrived(0)
     split(0, 0, lo)
@@ -327,6 +335,7 @@
     split(1, hi, depth // 2 - 1)
     correlate((0, rows), lead)
     outside(1)
+    gather(0)
     give(1)
     give(2)
     keep(1)
@@ -358,7 +367,7 @@
             out_ref[k, place] = top / jnp.sqrt(bottom)
             return carry
 
-        lax.fori_loop(0, velocities, velocity, 0)
+        lax.fori_loop(0, velocities, velocity, 0, unroll=4)
 
     @pl.when(early_goes)
     def _():

time: 35.2 us -> 35.6 us (1.011)
  Pallas kernels: 33.2 us -> 33.7 us
    pallas_call x1, Pallas kernels: 33.2 us -> 33.7 us  [shards(): pl.pallas_call(body, out_shape=jax.ShapeDtypeStruct((velocities, group //...]
where the time goes in v5:
time: 35.6 us; the launch traced here: 35.3 us
  Pallas kernels  33.7 us (95%)
  local copies, waits for them, and re-layouts  1.67 us (5%)
    pallas_call x1, Pallas kernels, shards(): pl.pallas_call(body, out_shape=jax.ShapeDtypeStruct((velocities, group //...  33.7 us
    unnamed x1, local copies, waits for them, and re-layouts  1.67 us

profile of v5, /device:TPU:24, one launch (start us, length us, event | category | flops | bytes accessed | tf_op | source)
XLA Modules:
  0.0 35.3 jit_solution(10549773829678975926)
XLA Ops:
  0.0 33.7 %shard_map.46 = f32[16,2,8,256]{3,2,1,0:T(8,128)} custom-call(f32[11,11]{1,0:T(8,128)} %refs_0_.1, s32[16,32]{1,0:T(8,128)} %bitcast.3, f32[8,64,256]{2,1,0:T(8,128)} %refs_2_.1, f32[8,64,256]{2,1,0:T(8,128)} %refs_3_.1), custom_call_target="tpu_custom_call" | custom-call | tf_op jit(solution)/shard_map/pallas_call | solution.py:416
  33.7 1.7 %copy.6 = f32[16,16,256]{2,1,0:T(8,128)} copy(f32[16,16,256]{2,1,0:T(8,128)} %bitcast.2) | data formatting | bytes 524288

commit v6 on v5

--- a/solution.py
+++ b/solution.py
@@ -60,7 +60,7 @@
     low,
     bands,
     images,
-    outer,
+    spill,
     part_send,
     part_own,
     part_recv,
@@ -72,6 +72,8 @@
     core_recv_sem,
     x_send_sem,
     x_recv_sem,
+    spill_send_sem,
+    spill_recv_sem,
 ):
     visits, rows, cols = sci_ref.shape
     size = psf_ref.shape[0]
@@ -133,13 +135,6 @@
             raw_recv_sem.at[0, 0],
             above,
         ),
-        remote(
-            images.at[:, :, MAXOFF + 1],
-            outer.at[1],
-            raw_send_sem.at[0, 1],
-            raw_recv_sem.at[0, 1],
-            above,
-        ),
     ]
     down = [
         remote(
@@ -147,13 +142,6 @@
             raw.at[:, 0:halo],
             raw_send_sem.at[1, 0],
             raw_recv_sem.at[1, 0],
-            below,
-        ),
-        remote(
-            images.at[:, :, MAXOFF + blocks - 2],
-            outer.at[0],
-            raw_send_sem.at[1, 1],
-            raw_recv_sem.at[1, 1],
             below,
         ),
     ]
@@ -300,6 +288,32 @@
         def _():
             hop[stage].start()
 
+    def spread(way, slot):
+        source = MAXOFF + blocks - 2 - (blocks - 3) * way
+        wanted = 2 * MAXOFF * way - MAXOFF
+
+        def velocity(k, carry):
+            totals = [None, None]
+            for t in range(visits):
+                place = jnp.where(off_ref[k, me * visits + t] == wanted, source, 0)
+                for image in range(2):
+                    term = images[image, t, place]
+                    totals[image] = term if t == 0 else totals[image] + term
+            spill[slot, 0, k] = totals[0]
+            spill[slot, 1, k] = totals[1]
+            return carry
+
+        lax.fori_loop(0, velocities, velocity, 0, unroll=4)
+
+    def spill_copy(src, dst, device):
+        return remote(spill.at[src], spill.at[dst], spill_send_sem.at[dst - 2], spill_recv_sem.at[dst - 2], device)
+
+    spill_core = spill_copy(0, 2, mate)
+    spill_hop = spill_copy(1, 3, across)
+    spill_on = spill_copy(1, 4, (sky + 1 - 2 * near, me))
+    passes = jnp.logical_and(early_goes, jnp.where(near == 0, has_below, has_above))
+    takes = jnp.where(near == 0, has_above, has_below)
+
     def arrived(chunk):
         @pl.when(has_above)
         def _():
@@ -324,9 +338,25 @@
     split(0, lo, hi)
     split(1, lo, hi)
     correlate((lead,), rows + 2 * BR - 2 * lead)
-    depart(1)
+    images[:, :, 0] = jnp.zeros((2, visits, BR, cols), F32)
+    images[:, :, blocks + 2 * MAXOFF - 1] = jnp.zeros((2, visits, BR, cols), F32)
+    spread(1 - near, 0)
+    spill_core.start()
+    spread(near, 1)
     give(0)
     keep(0)
+    spill_core.wait_recv()
+
+    def join(k, carry):
+        for image in range(2):
+            spill[1, image, k] += spill[2, image, k]
+        return carry
+
+    lax.fori_loop(0, velocities, join, 0, unroll=4)
+
+    @pl.when(jnp.logical_not(early_goes))
+    def _():
+        spill_hop.start()
 
     arrived(0)
     split(0, 0, lo)
@@ -335,6 +365,16 @@
     split(1, hi, depth // 2 - 1)
     correlate((0, rows), lead)
     outside(1)
+
+    @pl.when(early_goes)
+    def _():
+        spill_hop.wait_recv()
+        spill[1] += spill[3]
+
+    @pl.when(passes)
+    def _():
+        spill_on.start()
+
     gather(0)
     give(1)
     give(2)
@@ -343,17 +383,6 @@
     keep(2)
     gather(2)
 
-    arrived(1)
-
-    @pl.when(has_above)
-    def _():
-        images[:, :, 0] = outer[0]
-
-    @pl.when(has_below)
-    def _():
-        images[:, :, blocks + 2 * MAXOFF - 1] = outer[1]
-
-    outside(0)
     give(3)
     keep(3)
     gather(3)
@@ -372,6 +401,12 @@
     @pl.when(early_goes)
     def _():
         finish(2, 1 - near)
+
+        @pl.when(takes)
+        def _():
+            spill_on.wait_recv()
+            part_own[3] += spill[4]
+
         finish(3, near)
 
     @pl.when(jnp.logical_not(early_goes))
@@ -379,7 +414,7 @@
         finish(0, near)
         finish(1, 1 - near)
 
-    for chunk in range(2):
+    for chunk in range(1):
 
         @pl.when(has_above)
         def _():
@@ -393,6 +428,15 @@
         core[stage].wait_send()
     hop[0].wait_send()
     hop[1].wait_send()
+    spill_core.wait_send()
+
+    @pl.when(jnp.logical_not(early_goes))
+    def _():
+        spill_hop.wait_send()
+
+    @pl.when(passes)
+    def _():
+        spill_on.wait_send()
 
 
 def solution(mesh):
@@ -426,7 +470,7 @@
                 pltpu.VMEM((2, 2, depth // 2, 2 * visits, cols), BF16),
                 pltpu.VMEM((2, 2, size, cols, cols), BF16),
                 pltpu.VMEM((2, visits, rows // BR + 2 * MAXOFF, BR, cols), F32),
-                pltpu.VMEM((2, 2, visits, BR, cols), F32),
+                pltpu.VMEM((5,) + parts[1:], F32),
                 pltpu.VMEM(parts, F32),
                 pltpu.VMEM(parts, F32),
                 pltpu.VMEM(parts, F32),
@@ -438,6 +482,8 @@
                 dma((4,)),
                 dma((2,)),
                 dma((2,)),
+                dma((3,)),
+                dma((3,)),
             ],
             compiler_params=pltpu.CompilerParams(
                 collective_id=0, has_side_effects=True, vmem_limit_bytes=63 * 1024 * 1024

time: 35.6 us -> 32.9 us (0.924)
  Pallas kernels: 33.7 us -> 30.9 us
    pallas_call x1, Pallas kernels: 33.7 us -> 30.9 us  [shards(): pl.pallas_call(body, out_shape=jax.ShapeDtypeStruct((velocities, group //...]
where the time goes in v6:
time: 32.9 us; the launch traced here: 32.6 us
  Pallas kernels  30.9 us (94%)
  local copies, waits for them, and re-layouts  1.67 us (5%)
    pallas_call x1, Pallas kernels, shards(): pl.pallas_call(body, out_shape=jax.ShapeDtypeStruct((velocities, group //...  30.9 us
    unnamed x1, local copies, waits for them, and re-layouts  1.67 us

profile of v6, /device:TPU:24, one launch (start us, length us, event | category | flops | bytes accessed | tf_op | source)
XLA Modules:
  0.0 32.6 jit_solution(6907273332859380706)
XLA Ops:
  0.0 30.9 %shard_map.46 = f32[16,2,8,256]{3,2,1,0:T(8,128)} custom-call(f32[11,11]{1,0:T(8,128)} %refs_0_.1, s32[16,32]{1,0:T(8,128)} %bitcast.3, f32[8,64,256]{2,1,0:T(8,128)} %refs_2_.1, f32[8,64,256]{2,1,0:T(8,128)} %refs_3_.1), custom_call_target="tpu_custom_call" | custom-call | tf_op jit(solution)/shard_map/pallas_call | solution.py:460
  31.0 1.7 %copy.6 = f32[16,16,256]{2,1,0:T(8,128)} copy(f32[16,16,256]{2,1,0:T(8,128)} %bitcast.2) | data formatting | bytes 524288

commit v7 on v6

--- a/solution.py
+++ b/solution.py
@@ -359,21 +359,22 @@
         spill_hop.start()
 
     arrived(0)
+
+    @pl.when(early_goes)
+    def _():
+        spill_hop.wait_recv()
+        spill[1] += spill[3]
+
+    @pl.when(passes)
+    def _():
+        spill_on.start()
+
     split(0, 0, lo)
     split(1, 0, lo)
     split(0, hi, depth // 2)
     split(1, hi, depth // 2 - 1)
     correlate((0, rows), lead)
     outside(1)
-
-    @pl.when(early_goes)
-    def _():
-        spill_hop.wait_recv()
-        spill[1] += spill[3]
-
-    @pl.when(passes)
-    def _():
-        spill_on.start()
 
     gather(0)
     give(1)

time: 32.9 us -> 34.8 us (1.058)
  the two profiles are of different devices: /device:TPU:24 before, /device:TPU:0 now
where the time goes in v7:
time: 34.8 us; the launch traced here: 34.5 us
  Pallas kernels  32.8 us (94%)
  local copies, waits for them, and re-layouts  1.67 us (5%)
    pallas_call x1, Pallas kernels, shards(): pl.pallas_call(body, out_shape=jax.ShapeDtypeStruct((velocities, group //...  32.8 us
    unnamed x1, local copies, waits for them, and re-layouts  1.67 us

profile of v7, /device:TPU:0, one launch (start us, length us, event | category | flops | bytes accessed | tf_op | source)
XLA Modules:
  0.0 34.5 jit_solution(3645039396844728685)
XLA Ops:
  0.0 32.8 %shard_map.46 = f32[16,2,8,256]{3,2,1,0:T(8,128)} custom-call(f32[11,11]{1,0:T(8,128)} %refs_0_.1, s32[16,32]{1,0:T(8,128)} %bitcast.3, f32[8,64,256]{2,1,0:T(8,128)} %refs_2_.1, f32[8,64,256]{2,1,0:T(8,128)} %refs_3_.1), custom_call_target="tpu_custom_call" | custom-call | tf_op jit(solution)/shard_map/pallas_call | solution.py:461
  32.8 1.7 %copy.6 = f32[16,16,256]{2,1,0:T(8,128)} copy(f32[16,16,256]{2,1,0:T(8,128)} %bitcast.2) | data formatting | bytes 524288

commit v8 on v6

--- a/solution.py
+++ b/solution.py
@@ -358,6 +358,7 @@
     def _():
         spill_hop.start()
 
+    gather(0)
     arrived(0)
     split(0, 0, lo)
     split(1, 0, lo)
@@ -375,7 +376,6 @@
     def _():
         spill_on.start()
 
-    gather(0)
     give(1)
     give(2)
     keep(1)

time: 32.9 us -> 32.9 us (level)
  the two profiles are of different devices: /device:TPU:24 before, /device:TPU:0 now
where the time goes in v8:
time: 32.9 us; the launch traced here: 32.6 us
  Pallas kernels  30.9 us (94%)
  local copies, waits for them, and re-layouts  1.67 us (5%)
    pallas_call x1, Pallas kernels, shards(): pl.pallas_call(body, out_shape=jax.ShapeDtypeStruct((velocities, group //...  30.9 us
    unnamed x1, local copies, waits for them, and re-layouts  1.67 us

profile of v8, /device:TPU:0, one launch (start us, length us, event | category | flops | bytes accessed | tf_op | source)
XLA Modules:
  0.0 32.6 jit_solution(2419953236460763975)
XLA Ops:
  0.0 30.9 %shard_map.46 = f32[16,2,8,256]{3,2,1,0:T(8,128)} custom-call(f32[11,11]{1,0:T(8,128)} %refs_0_.1, s32[16,32]{1,0:T(8,128)} %bitcast.3, f32[8,64,256]{2,1,0:T(8,128)} %refs_2_.1, f32[8,64,256]{2,1,0:T(8,128)} %refs_3_.1), custom_call_target="tpu_custom_call" | custom-call | tf_op jit(solution)/shard_map/pallas_call | solution.py:460
  30.9 1.7 %copy.6 = f32[16,16,256]{2,1,0:T(8,128)} copy(f32[16,16,256]{2,1,0:T(8,128)} %bitcast.2) | data formatting | bytes 524288
